TPU v7x, 512 devices: a whole 4x8x8 slice. The times are simulated.
512 devices in a mesh: dp: 16 (over z, x_hi), chan: 2 (over core), tm: 16 (over y, x_lo).
Axes of the slice: x: 4 (x_hi: 2, x_lo: 2; x = x_hi * 2 + x_lo), y: 8, z: 8, core: 2. Of those that a mesh axis runs over, the one named last changes fastest.
Arguments:
- inputs: bfloat16 [16, 2, 2048, 1536], P('dp', 'chan', 'tm'), may hold values from -6 to 6
- out_grad: bfloat16 [16, 2, 2048, 1536], P('dp', 'chan', 'tm'), may hold values from -6 to 6
- proj_weight: bfloat16 [1536, 3072], P(('dp', 'chan')), may hold values from -0.15625 to 0.15625
- conv_kernel: float32 [31, 1536], replicated, may hold values from -1 to 1
- norm_mean: float32 [1536], replicated, may hold values from -0.5 to 0.5
- norm_var: float32 [1536], replicated, may hold values from 0.1 to 1
- norm_gain: float32 [1536], replicated, may hold values from 0.1 to 1.9
- norm_bias: float32 [1536], replicated, may hold values from -0.5 to 0.5
- lengths: int32 [16], P('dp'), may hold values from 512 to 2048, as said below
Outputs:
- input_grad: bfloat16 [16, 2, 2048, 1536], P('dp', 'chan', 'tm')
- kernel_grad: float32 [31, 1536], replicated
- gain_grad: float32 [1536], replicated
- bias_grad: float32 [1536], replicated
Inputs may be any that keep to these rules, and one draw needn't show every extreme that they name: `lengths`: valid frames of each segment; at least one segment has all 2048.
All inputs are finite; a program needn't handle non-finite values.
Results may differ from a plain program's by a relative error of at most 0.0062.
Values may be sent and summed in bfloat16 or wider, within the bound.
A program may use at most 64 MiB of HBM per device.

v0:
```python
import jax
import jax.numpy as jnp
from jax import lax
from jax.sharding import PartitionSpec as P

KERNEL = 31


def padded(block, sides, width):
    for axis, dim in sides:
        count = lax.axis_size(axis)
        forward = [(i, i + 1) for i in range(count - 1)]
        backward = [(target, source) for source, target in forward]
        low = lax.ppermute(
            lax.slice_in_dim(block, block.shape[dim] - width, None, axis=dim), axis, forward
        )
        high = lax.ppermute(lax.slice_in_dim(block, 0, width, axis=dim), axis, backward)
        block = jnp.concatenate([low, block, high], axis=dim)
    return block


def gate_units(pre, keep, width):
    value = pre[:, :width]
    gate = jax.nn.sigmoid(pre[:, width:])
    return (value * gate * keep).astype(jnp.bfloat16)


def per_device(
    inputs, out_grad, proj_weight, conv_kernel, norm_mean, norm_var, norm_gain, norm_bias, lengths
):
    frames = inputs.shape[2]
    width = inputs.shape[3]
    half = KERNEL // 2
    rows = inputs.reshape(frames, width)
    start = lax.axis_index("tm") * frames
    limit = lengths[0]
    weight = lax.all_gather(proj_weight, ("dp", "chan"), axis=0, tiled=True)
    place = start + jnp.arange(frames)
    keep = (place < limit).astype(jnp.float32)[:, None]
    pre = jnp.dot(rows, weight, preferred_element_type=jnp.float32)
    gated = gate_units(pre, keep, width)
    gated_ext = padded(gated, (("tm", 0),), half)
    gated_wide = gated_ext.astype(jnp.float32)
    conv = jnp.zeros((frames, width), jnp.float32)
    for k in range(KERNEL):
        conv = conv + conv_kernel[k] * gated_wide[k : k + frames]
    rstd = 1.0 / jnp.sqrt(norm_var + 1e-05)
    normed = (conv - norm_mean) * rstd
    act = normed * norm_gain + norm_bias
    sig = jax.nn.sigmoid(act)
    act_grad = (
        out_grad.reshape(frames, width).astype(jnp.float32) * keep * sig * (1.0 + act * (1.0 - sig))
    )
    conv_grad = (act_grad * norm_gain * rstd).astype(jnp.bfloat16)
    gain_part = jnp.sum(act_grad * normed, axis=0)
    bias_part = jnp.sum(act_grad, axis=0)
    conv_grad_f = conv_grad.astype(jnp.float32)
    kernel_part = jnp.stack(
        [jnp.sum(conv_grad_f * gated_wide[k : k + frames], axis=0) for k in range(KERNEL)]
    )
    grad_ext = padded(conv_grad, (("tm", 0),), half).astype(jnp.float32)
    gated_grad = jnp.zeros((frames, width), jnp.float32)
    for k in range(KERNEL):
        gated_grad = gated_grad + conv_kernel[k] * grad_ext[2 * half - k : 2 * half - k + frames]
    gated_grad = gated_grad * keep
    value = pre[:, :width]
    gate = jax.nn.sigmoid(pre[:, width:])
    pre_grad = jnp.concatenate(
        [gated_grad * gate, gated_grad * value * gate * (1.0 - gate)], axis=1
    ).astype(jnp.bfloat16)
    input_grad = jnp.dot(pre_grad, weight.T, preferred_element_type=jnp.float32).astype(
        jnp.bfloat16
    )
    kernel_sum, gain_sum, bias_sum = lax.psum(
        (kernel_part, gain_part, bias_part), ("dp", "chan", "tm")
    )
    total = lax.axis_size("dp") * lax.axis_size("chan") * lax.axis_size("tm") * frames
    scale = 1.0 / jnp.sqrt(jnp.float32(total))
    return (
        input_grad.reshape(1, 1, frames, width),
        kernel_sum * scale,
        gain_sum * scale,
        bias_sum * scale,
    )


def solution(mesh):
    in_specs = (
        P("dp", "chan", "tm", None),
        P("dp", "chan", "tm", None),
        P(("dp", "chan"), None),
        P(),
        P(),
        P(),
        P(),
        P(),
        P("dp"),
    )
    out_specs = (P("dp", "chan", "tm", None), P(), P(), P())
    return jax.shard_map(
        per_device, mesh=mesh, in_specs=in_specs, out_specs=out_specs, check_vma=False
    )
```

profile of v0, /device:TPU:1, one launch (start us, length us, event | category | flops | bytes accessed | tf_op | source)
XLA Modules:
  0.0 424.9 jit_solution(6434605158560623436)
XLA Ops:
  7.2 0.0 copy-start
  7.2 0.0 all-gather.2.cloned.1.call-start
  7.2 0.7 all-gather.2.cloned.1.call-update
  7.9 0.0 all-reduce.3.cloned.1.call-start
  8.6 1.9 slice_reduce_fusion.30
  10.5 0.7 add_rsqrt_fusion
  11.2 117.5 %all-gather.2.cloned.1.call-done = bf16[1536,3072]{1,0:T(8,128)(2,1)} async-done(((bf16[48,3072]{1,0:T(8,128)(2,1)}), bf16[1536,3072]{1,0:T(8,128)(2,1)}) %all-gather.2.cloned.1.call-update) | async-done | bytes 9437200 | tf_op jit(solution)/shard_map/all_gather | solution.py:37
  128.7 0.0 copy-done
  128.7 5.1 %fusion.71 = f32[128,3072]{1,0:T(8,128)S(1)} fusion(bf16[1536,3072]{1,0:T(8,128)(2,1)} %all-gather.2.cloned.1.call-done, bf16[1,1,128,1536]{3,2,1,0:T(8,128)(2,1)S(1)} %copy-done), kind=kOutput, calls=%fused_computation.144 | convolution fusion | flops 1207959552 | bytes 11403264 | tf_op jit(solution)/shard_map/dot_general | solution.py:40
  133.8 0.0 copy-start.1
  133.8 0.0 copy-start.2
  133.8 0.0 copy-start.3
  133.8 0.0 copy-start.4
  133.8 0.2 multiply_convert_fusion.3
  134.1 2.2 collective-permute-start
  136.3 1.3 collective-permute-start.1
  137.6 1.4 slice_reduce_fusion.29
  139.0 0.0 collective-permute-done
  139.0 2.8 collective-permute-done.1
  141.8 0.1 maximum_convert_fusion
  141.9 0.0 copy-done.1
  141.9 0.0 copy-done.2
  141.9 0.0 copy-done.3
  141.9 0.0 copy-done.4
  142.0 3.6 fusion.74
  145.6 2.1 fusion.31
  147.6 1.2 fusion.30
  149.3 2.8 stack.127
  152.1 0.0 all-reduce.3.cloned.1.call-update
  152.1 4.3 %collective-permute-start.2 = (bf16[15,1536]{1,0:T(8,128)(2,1)S(1)}, bf16[15,1536]{1,0:T(8,128)(2,1)S(1)}, u32[]{:S(2)}, u32[]{:S(2)}) collective-permute-start(bf16[15,1536]{1,0:T(8,128)(2,1)S(1)} %get-tuple-element.74), channel_id=1, source_target_pairs={{0,1},{1,2},{2,3},{3,4},{4,5},{5,6},{6,7},{7,8},{8,9},{9,10},{10,1... | collective-permute-start | bytes 138248 | tf_op jit(solution)/shard_map/ppermute | solution.py:14
  156.4 1.3 collective-permute-start.3
  157.7 100.3 %all-reduce = (f32[1536]{0:T(1024)S(1)}, f32[1536]{0:T(1024)S(1)}) all-reduce(f32[1536]{0:T(1024)S(1)} %get-tuple-element.36, f32[1536]{0:T(1024)S(1)} %get-tuple-element.35), channel_id=1, replica_groups=mesh['dp'=16,'chan'=2,'tm'=16] {'dp','chan','tm'}, use_global_device_ids=true, to_apply=%region_33.0 | all-reduce | flops 3072 | bytes 24576 | tf_op jit(solution)/shard_map/psum | solution.py:74
  258.0 0.6 broadcast_multiply_fusion.1
  258.6 0.0 collective-permute-done.2
  258.6 0.0 collective-permute-done.3
  258.6 0.0 slice-start
  258.6 0.1 maximum_convert_fusion.1
  258.7 0.0 slice-start.1
  258.7 0.0 slice-start.2
  258.7 3.3 multiply_convert_fusion.1
  262.0 0.3 multiply_convert_fusion
  262.3 0.0 slice-done
  262.3 0.0 slice-done.1
  262.3 0.0 slice-done.2
  262.3 4.0 fusion
  266.3 150.1 %all-reduce.3.cloned.1.call-done = f32[31,1536]{1,0:T(8,128)} async-done(((f32[31,1536]{1,0:T(8,128)}), f32[31,1536]{1,0:T(8,128)}) %all-reduce.3.cloned.1.call-update) | async-done | bytes 190480 | tf_op jit(solution)/shard_map/psum | solution.py:74
  416.5 1.6 broadcast_multiply_fusion
  (35 shorter events, 0.2 us)
Async XLA Ops:
  7.2 121.5 %copy-start = (bf16[1,1,128,1536]{3,2,1,0:T(8,128)(2,1)S(1)}, bf16[1,1,128,1536]{3,2,1,0:T(8,128)(2,1)}, u32[]{:S(2)}) copy-start(bf16[1,1,128,1536]{3,2,1,0:T(8,128)(2,1)} %param.9) | copy-start | bytes 1179652
  7.2 121.5 %all-gather.2.cloned.1.call-start = ((), (), s32[]{:S(2)}) async-start(), calls=%async_computation | async-start | bytes 9732096 | tf_op jit(solution)/shard_map/all_gather | solution.py:37
  7.9 408.5 %all-reduce.3.cloned.1.call-start = ((), (), s32[]{:S(2)}) async-start(), calls=%async_computation.1 | async-start | bytes 393216 | tf_op jit(solution)/shard_map/psum | solution.py:74
  133.8 8.1 %copy-start.1 = (bf16[1,1,128,1536]{3,2,1,0:T(8,128)(2,1)S(1)}, bf16[1,1,128,1536]{3,2,1,0:T(8,128)(2,1)}, u32[]{:S(2)}) copy-start(bf16[1,1,128,1536]{3,2,1,0:T(8,128)(2,1)} %param.10) | copy-start | bytes 1179652
  133.8 8.1 %copy-start.2 = (f32[1536]{0:T(1024)S(1)}, f32[1536]{0:T(1024)}, u32[]{:S(2)}) copy-start(f32[1536]{0:T(1024)} %param.15) | copy-start | bytes 18436
  133.8 8.1 %copy-start.3 = (f32[1536]{0:T(1024)S(1)}, f32[1536]{0:T(1024)}, u32[]{:S(2)}) copy-start(f32[1536]{0:T(1024)} %param.16) | copy-start | bytes 18436
  133.8 8.1 %copy-start.4 = (f32[1536]{0:T(1024)S(1)}, f32[1536]{0:T(1024)}, u32[]{:S(2)}) copy-start(f32[1536]{0:T(1024)} %param.13) | copy-start | bytes 18436
  134.1 4.9 %collective-permute-start = (bf16[15,1536]{1,0:T(8,128)(2,1)S(1)}, bf16[15,1536]{1,0:T(8,128)(2,1)S(1)}, u32[]{:S(2)}, u32[]{:S(2)}) collective-permute-start(bf16[15,1536]{1,0:T(8,128)(2,1)S(1)} %get-tuple-element.76), channel_id=1, source_target_pairs={{0,1},{1,2},{2,3},{3,4},{4,5},{5,6},{6,7},{7,8},{8,9},{9,10},{10,1... | collective-permute-start | bytes 138248 | tf_op jit(solution)/shard_map/ppermute | solution.py:14
  136.3 5.5 %collective-permute-start.1 = (bf16[15,1536]{1,0:T(8,128)(2,1)S(1)}, bf16[15,1536]{1,0:T(8,128)(2,1)S(1)}, u32[]{:S(2)}, u32[]{:S(2)}) collective-permute-start(bf16[15,1536]{1,0:T(8,128)(2,1)S(1)} %get-tuple-element.77), channel_id=1, source_target_pairs={{1,0},{2,1},{3,2},{4,3},{5,4},{6,5},{7,6},{8,7},{9,8},{10,9},{11,1... | collective-permute-start | bytes 138248 | tf_op jit(solution)/shard_map/ppermute | solution.py:17
  152.1 106.5 %collective-permute-start.2 = (bf16[15,1536]{1,0:T(8,128)(2,1)S(1)}, bf16[15,1536]{1,0:T(8,128)(2,1)S(1)}, u32[]{:S(2)}, u32[]{:S(2)}) collective-permute-start(bf16[15,1536]{1,0:T(8,128)(2,1)S(1)} %get-tuple-element.74), channel_id=1, source_target_pairs={{0,1},{1,2},{2,3},{3,4},{4,5},{5,6},{6,7},{7,8},{8,9},{9,10},{10,1... | collective-permute-start | bytes 138248 | tf_op jit(solution)/shard_map/ppermute | solution.py:14
  156.4 102.2 %collective-permute-start.3 = (bf16[15,1536]{1,0:T(8,128)(2,1)S(1)}, bf16[15,1536]{1,0:T(8,128)(2,1)S(1)}, u32[]{:S(2)}, u32[]{:S(2)}) collective-permute-start(bf16[15,1536]{1,0:T(8,128)(2,1)S(1)} %get-tuple-element.75), channel_id=1, source_target_pairs={{1,0},{2,1},{3,2},{4,3},{5,4},{6,5},{7,6},{8,7},{9,8},{10,9},{11,1... | collective-permute-start | bytes 138248 | tf_op jit(solution)/shard_map/ppermute | solution.py:17
  258.6 3.7 slice-start
  258.7 3.6 slice-start.1
  258.7 3.6 slice-start.2
Sparse Core Ops, SparseCore 0:
  11.4 117.2 all-gather.1
  152.2 264.2 all-reduce.2
where the time goes:
time: 425 us
  waiting for transfers between devices  271 us (64%)
  blocking collectives  100 us (24%)
  between operations  15.2 us (4%)
  other arithmetic  13.8 us (3%)
  starting transfers between devices  9.12 us (2%)
  matrix products  9.07 us (2%)
  local copies, waits for them, and re-layouts  6.31 us (1%)
    psum x1, waiting for transfers between devices, per_device(): lax.psum((kernel_part, gain_part, bias_part), ('dp', 'chan', 'tm'))  150 us
    all_gather x1, waiting for transfers between devices, per_device(): weight = lax.all_gather(proj_weight, ('dp', 'chan'), axis=0, tiled=True)  117 us
    psum x1, blocking collectives, per_device(): lax.psum((kernel_part, gain_part, bias_part), ('dp', 'chan', 'tm'))  100 us
  transfers between devices with their start and end apart: 6, of which 3 were waited for; matrix products, arithmetic and copies ran while one was open for 3% of the time, Pallas kernels for 0%

commit v1 on v0

v1 whole, which is shorter than its diff:
```python
import functools

import jax
import jax.numpy as jnp
from jax import lax
from jax.experimental import pallas as pl
from jax.experimental.pallas import tpu as pltpu
from jax.sharding import PartitionSpec as P

MESH = pl.DeviceIdType.MESH
D = 1536
KERNEL = 31
FRAMES = 2048
ROWS = 128
HALO = 32
GHALO = 16
WIDE = ROWS + 2 * HALO
MID = ROWS + 2 * GHALO
SHARD = 48
CW = 128
CHUNKS = D // CW
DP, CHAN, TM = 16, 2, 16
GROUP = TM * CHAN
PART = 24
F32 = jnp.float32
BF16 = jnp.bfloat16
GROUPS = ((0, 6), (6, 12))


def copy_to(src, dst, send, recv, device):
    return pltpu.make_async_remote_copy(
        src_ref=src, dst_ref=dst, send_sem=send, recv_sem=recv, device_id=device, device_id_type=MESH
    )


def await_bytes(ref, sem):
    pltpu.make_async_copy(ref, ref, sem).wait()


def kernel(
    limit, x_in, og_in, w_in, ck, mean, var, gain, bias,
    out, kernel_out, gain_out, bias_out,
    wg, xe, oe, gw, cg, pre, pgr, acc, parts, rb1, rb2, res,
    halo_send, halo_recv, opp_send, opp_recv, z_send, z_recv, y_send, y_recv, s_send, s_recv,
    r1_send, r1_recv, r2_send, r2_recv, r3_send, r3_recv,
):
    dp, c, tm = lax.axis_index("dp"), lax.axis_index("chan"), lax.axis_index("tm")
    z, y = dp // 2, tm // 2
    opp_dp = dp + 1 - 2 * (dp % 2)
    opp_tm = tm + 1 - 2 * (tm % 2)
    me = tm * CHAN + c
    hb = y % 2

    barrier = pltpu.get_barrier_semaphore()

    def greet(i, carry):
        other = lax.rem(me + i, GROUP)
        pl.semaphore_signal(
            barrier, inc=1, device_id=(dp, other % 2, other // 2), device_id_type=MESH
        )
        return carry

    def greet_dp(i, carry):
        pl.semaphore_signal(
            barrier, inc=1, device_id=(lax.rem(dp + i, DP), c, tm), device_id_type=MESH
        )
        return carry

    lax.fori_loop(1, GROUP, greet, 0)
    lax.fori_loop(1, DP, greet_dp, 0)
    pl.semaphore_signal(barrier, inc=1, device_id=(opp_dp, c, opp_tm), device_id_type=MESH)

    for j in range(CHUNKS):
        wg[j, hb, dp, c] = w_in[:, pl.ds(pl.multiple_of(hb * D + j * CW, CW), CW)]
    xe[HALO : HALO + ROWS] = x_in[...]
    oe[GHALO : GHALO + ROWS] = og_in[...]
    pl.semaphore_wait(barrier, GROUP + DP - 1)

    for g, (lo, hi) in enumerate(GROUPS):
        here = wg.at[lo:hi, hb, dp, c]
        copy_to(here, here, opp_send.at[g], opp_recv.at[g], (opp_dp, c, opp_tm)).start()

    right, left = (dp, c, lax.rem(tm + 1, TM)), (dp, c, lax.rem(tm + TM - 1, TM))
    halos = (
        copy_to(x_in.at[ROWS - HALO :], xe.at[0:HALO], halo_send.at[0], halo_recv.at[0], right),
        copy_to(x_in.at[0:HALO], xe.at[HALO + ROWS :], halo_send.at[1], halo_recv.at[1], left),
        copy_to(og_in.at[ROWS - GHALO :], oe.at[0:GHALO], halo_send.at[2], halo_recv.at[2], right),
        copy_to(og_in.at[0:GHALO], oe.at[GHALO + ROWS :], halo_send.at[3], halo_recv.at[3], left),
    )
    for h in halos:
        h.start()

    up = (lax.rem(dp + 2, DP), c, tm)
    down = (lax.rem(dp + DP - 2, DP), c, tm)
    y_even = y + 1 - 2 * (y % 2)
    y_odd = lax.rem(y + 7 + 2 * (y % 2), 8)
    y_partner = tuple((dp, c, p * 2 + tm % 2) for p in (y_even, y_odd))

    def pair(j, zz, h=None):
        return wg.at[j, hb if h is None else h, pl.ds(2 * lax.rem(zz + 8, 8), 2), c]

    def ring_step(j, parity, s):
        ups, downs = (4, 3) if parity == 0 else (3, 4)
        for d, (steps, sign, device) in enumerate(((ups, -1, up), (downs, 1, down))):
            if s > steps:
                continue
            block = pair(j, z + sign * s)
            if s > 0:
                await_bytes(block, z_recv.at[d, j, s - 1])
            if s < steps:
                copy_to(block, block, z_send.at[j], z_recv.at[d, j, s], device).start()
            if s > 0 or d == 0:
                copy_to(block, block, y_send.at[j], y_recv.at[j], y_partner[parity]).start()

    for g, (lo, hi) in enumerate(GROUPS):
        there = wg.at[lo:hi, hb, opp_dp, c]
        await_bytes(there, opp_recv.at[g])
        for s in range(5):

            def both(i, carry):
                for parity in range(2):
                    ring_step(lo + 2 * i + parity, parity, s)
                return carry

            lax.fori_loop(0, (hi - lo) // 2, both, 0)

    def relay(j, carry):
        await_bytes(wg.at[j, 1 - hb, :, c], y_recv.at[j])
        mine = wg.at[j, :, :, c]
        copy_to(mine, mine, s_send.at[j], s_recv.at[j], (dp, 1 - c, tm)).start()
        return carry

    lax.fori_loop(0, CHUNKS, relay, 0)
    for h in halos:
        h.wait()

    t = lax.broadcasted_iota(jnp.int32, (WIDE, CW), 0) + (tm * ROWS - HALO)
    keep = ((t >= 0) & (t < limit[0])).astype(F32)
    keep_mid = keep[HALO - GHALO : HALO + ROWS + GHALO]
    acc[...] = jnp.zeros_like(acc)

    def chunk(j, carry):
        await_bytes(wg.at[j, :, :, 1 - c], s_recv.at[j])
        cs = pl.ds(pl.multiple_of(j * CW, CW), CW)
        w = jnp.concatenate([wg[j, h].reshape(D, CW) for h in range(2)], axis=1)
        pre[...] = jnp.dot(xe[...], w, preferred_element_type=F32)
        sg = lax.logistic(pre[:, CW:])
        gw[...] = (pre[:, :CW] * sg * keep).astype(BF16).astype(F32)
        pre[:, CW:] = sg
        rstd = 1.0 / jnp.sqrt(var[0:1, cs] + 1e-05)
        scale = gain[0:1, cs] * rstd
        gs = jnp.zeros((8, CW), F32)
        bs = jnp.zeros((8, CW), F32)
        step = 80
        for r in range(0, MID, step):
            a = jnp.zeros((step, CW), F32)
            for k in range(KERNEL):
                a = a + ck[k : k + 1, cs] * gw[r + k + 1 : r + k + 1 + step, :]
            normed = (a - mean[0:1, cs]) * rstd
            act = normed * gain[0:1, cs] + bias[0:1, cs]
            sig = lax.logistic(act)
            ag = oe[r : r + step, cs].astype(F32) * keep_mid[r : r + step] * sig
            ag = ag * (1.0 + act * (1.0 - sig))
            cg[r : r + step] = (ag * scale).astype(BF16).astype(F32)
            lo, hi = max(r, GHALO) - r, min(r + step, GHALO + ROWS) - r
            gs = gs + jnp.sum((ag * normed)[lo:hi].reshape((hi - lo) // 8, 8, CW), axis=0)
            bs = bs + jnp.sum(ag[lo:hi].reshape((hi - lo) // 8, 8, CW), axis=0)
        own = cg[GHALO : GHALO + ROWS]
        for k in range(KERNEL):
            s = jnp.sum(own * gw[k + 17 : k + 17 + ROWS], axis=0, keepdims=True)
            parts[j, k // PART, k % PART : k % PART + 1] = s
        parts[j, 1, 7:8] = jnp.sum(gs, axis=0, keepdims=True)
        parts[j, 1, 8:9] = jnp.sum(bs, axis=0, keepdims=True)
        parts[j, 1, 9:] = jnp.zeros((PART - 9, CW), F32)
        step = 64
        for r in range(0, ROWS, step):
            a = jnp.zeros((step, CW), F32)
            for k in range(KERNEL):
                a = a + ck[k : k + 1, cs] * cg[r + 31 - k : r + 31 - k + step]
            a = a * keep_mid[GHALO + r : GHALO + r + step]
            value = pre[HALO + r : HALO + r + step, :CW]
            sg = pre[HALO + r : HALO + r + step, CW:]
            a = a * sg
            pgr[r : r + step, :CW] = a.astype(BF16)
            pgr[r : r + step, CW:] = (a * value * (1.0 - sg)).astype(BF16)
        acc[...] += lax.dot_general(
            pgr[...], w, (((1,), (1,)), ((), ())), preferred_element_type=F32
        )
        for piece in range(2):
            home = (tm == j) & (c == piece)

            @pl.when(home)
            def _():
                rb1[me] = parts[j, piece]

            @pl.when(jnp.logical_not(home))
            def _():
                copy_to(
                    parts.at[j, piece], rb1.at[me], r1_send.at[j, piece], r1_recv, (dp, piece, j)
                ).start()

        return carry

    lax.fori_loop(0, CHUNKS, chunk, 0)
    out[...] = acc[...].astype(BF16)

    @pl.when(tm < CHUNKS)
    def _():
        await_bytes(rb1.at[0 : GROUP - 1], r1_recv)
        total = rb1[0]
        for i in range(1, GROUP):
            total = total + rb1[i]
        rb2[dp] = total

        def spread(i, carry):
            copy_to(
                rb2.at[dp], rb2.at[dp], r2_send.at[i], r2_recv, (lax.rem(dp + i, DP), c, tm)
            ).start()
            return carry

        lax.fori_loop(1, DP, spread, 0)
        await_bytes(rb2.at[0 : DP - 1], r2_recv)
        total = rb2[0]
        for i in range(1, DP):
            total = total + rb2[i]
        res[tm, c] = total * (1.0 / 256.0)

        def share(i, carry):
            other = lax.rem(me + i, GROUP)
            copy_to(
                res.at[tm, c], res.at[tm, c], r3_send.at[i], r3_recv.at[tm, c],
                (dp, other % 2, other // 2),
            ).start()
            return carry

        lax.fori_loop(1, GROUP, share, 0)

    for j in range(CHUNKS):
        for piece in range(2):

            @pl.when(jnp.logical_not((tm == j) & (c == piece)))
            def _():
                await_bytes(res.at[j, piece], r3_recv.at[j, piece])
                await_bytes(parts.at[j, piece], r1_send.at[j, piece])

        cols = slice(j * CW, (j + 1) * CW)
        kernel_out[0:PART, cols] = res[j, 0]
        kernel_out[PART:KERNEL, cols] = res[j, 1, 0 : KERNEL - PART]
        gain_out[:, cols] = res[j, 1, 7:8]
        bias_out[:, cols] = res[j, 1, 8:9]

    for g, (lo, hi) in enumerate(GROUPS):
        await_bytes(wg.at[lo:hi, hb, dp, c], opp_send.at[g])

    def sent(j, carry):
        await_bytes(wg.at[j, 0, 0:14, 0], z_send.at[j])
        await_bytes(wg.at[j, 0, :, 0], y_send.at[j])
        await_bytes(wg.at[j, :, :, c], s_send.at[j])
        return carry

    lax.fori_loop(0, CHUNKS, sent, 0)

    @pl.when(tm < CHUNKS)
    def _():
        def done(i, carry):
            await_bytes(rb2.at[0], r2_send.at[i])
            return carry

        def done3(i, carry):
            await_bytes(res.at[0, 0], r3_send.at[i])
            return carry

        lax.fori_loop(1, DP, done, 0)
        lax.fori_loop(1, GROUP, done3, 0)


def per_device(
    inputs, out_grad, proj_weight, conv_kernel, norm_mean, norm_var, norm_gain, norm_bias, lengths
):
    vmem = pl.BlockSpec(memory_space=pltpu.VMEM)
    dma = pltpu.SemaphoreType.DMA
    row = lambda a: a.reshape(1, D)
    grad, kernel_grad, gain_grad, bias_grad = pl.pallas_call(
        kernel,
        out_shape=(
            jax.ShapeDtypeStruct((ROWS, D), BF16),
            jax.ShapeDtypeStruct((KERNEL, D), F32),
            jax.ShapeDtypeStruct((1, D), F32),
            jax.ShapeDtypeStruct((1, D), F32),
        ),
        in_specs=[pl.BlockSpec(memory_space=pltpu.SMEM)] + [vmem] * 8,
        out_specs=(vmem,) * 4,
        scratch_shapes=[
            pltpu.VMEM((CHUNKS, 2, DP, CHAN, SHARD, CW), BF16),
            pltpu.VMEM((WIDE, D), BF16),
            pltpu.VMEM((MID, D), BF16),
            pltpu.VMEM((WIDE, CW), F32),
            pltpu.VMEM((MID, CW), F32),
            pltpu.VMEM((WIDE, 2 * CW), F32),
            pltpu.VMEM((ROWS, 2 * CW), BF16),
            pltpu.VMEM((ROWS, D), F32),
            pltpu.VMEM((CHUNKS, 2, PART, CW), F32),
            pltpu.VMEM((GROUP, PART, CW), F32),
            pltpu.VMEM((DP, PART, CW), F32),
            pltpu.VMEM((CHUNKS, 2, PART, CW), F32),
            dma((4,)), dma((4,)),
            dma((len(GROUPS),)), dma((len(GROUPS),)),
            dma((CHUNKS,)), dma((2, CHUNKS, 4)),
            dma((CHUNKS,)), dma((CHUNKS,)),
            dma((CHUNKS,)), dma((CHUNKS,)),
            dma((CHUNKS, 2)), dma,
            dma((DP,)), dma,
            dma((GROUP,)), dma((CHUNKS, 2)),
        ],
        compiler_params=pltpu.CompilerParams(
            collective_id=0, has_side_effects=True, vmem_limit_bytes=48 << 20
        ),
    )(
        lengths, inputs.reshape(ROWS, D), out_grad.reshape(ROWS, D), proj_weight, conv_kernel,
        row(norm_mean), row(norm_var), row(norm_gain), row(norm_bias),
    )
    return (
        grad.reshape(1, 1, ROWS, D),
        kernel_grad,
        gain_grad.reshape(D),
        bias_grad.reshape(D),
    )


def solution(mesh):
    in_specs = (
        P("dp", "chan", "tm", None),
        P("dp", "chan", "tm", None),
        P(("dp", "chan"), None),
        P(),
        P(),
        P(),
        P(),
        P(),
        P("dp"),
    )
    out_specs = (P("dp", "chan", "tm", None), P(), P(), P())
    return jax.shard_map(
        per_device, mesh=mesh, in_specs=in_specs, out_specs=out_specs, check_vma=False
    )
```

time: 425 us -> 108 us (0.25)
  waiting for transfers between devices: 271 us -> 0 us
  blocking collectives: 100 us -> 0 us
  Pallas kernels: 0 us -> 98.1 us
  between operations: 15.2 us -> 1.31 us
  other arithmetic: 13.8 us -> 1.24 us
  starting transfers between devices: 9.12 us -> 0 us
  matrix products: 9.07 us -> 0 us
    psum x1 -> x0, waiting for transfers between devices: 150 us -> none  [per_device(): lax.psum((kernel_part, gain_part, bias_part), ('dp', 'chan', 'tm'))]
    all_gather x1 -> x0, waiting for transfers between devices: 117 us -> none  [per_device(): weight = lax.all_gather(proj_weight, ('dp', 'chan'), axis=0, tiled=True)]
    psum x1 -> x0, blocking collectives: 100 us -> none  [per_device(): lax.psum((kernel_part, gain_part, bias_part), ('dp', 'chan', 'tm'))]
    pallas_call x0 -> x1, Pallas kernels: none -> 98.1 us  [per_device(): pl.pallas_call(kernel, out_shape=(jax.ShapeDtypeStruct((ROWS, D), BF16),...]
    dot_general x2 -> x0, matrix products: 9.07 us -> none  [the longest x1 5.07 us: per_device(): pre = jnp.dot(rows, weight, preferred_element_type=jnp.float32)]
    ppermute x4 -> x0, starting transfers between devices: 9.04 us -> none  [the longest x2 6.46 us: padded(): lax.ppermute(lax.slice_in_dim(block, block.shape[dim] - width, None, axis...]
    reduce_sum x3 -> x0, other arithmetic: 6.87 us -> none  [the longest x1 3.62 us: per_device(): bias_part = jnp.sum(act_grad, axis=0)]
    unnamed x16, local copies, waits for them, and re-layouts: 0.05 us -> 6.67 us
  transfers between devices with their start and end apart: 6 -> 0, of which waited for: 3 -> 0; matrix products, arithmetic and copies ran while one was open for 3% -> 0% of each run, Pallas kernels for 0% -> 0%
where the time goes in v1:
time: 108 us
  Pallas kernels  98.1 us (91%)
  local copies, waits for them, and re-layouts  7.4 us (7%)
  between operations  1.31 us (1%)
  other arithmetic  1.24 us (1%)
    pallas_call x1, Pallas kernels, per_device(): pl.pallas_call(kernel, out_shape=(jax.ShapeDtypeStruct((ROWS, D), BF16),...  98.1 us
    unnamed x16, local copies, waits for them, and re-layouts  6.67 us

profile of v1, /device:TPU:1, one launch (start us, length us, event | category | flops | bytes accessed | tf_op | source)
XLA Modules:
  0.0 108.0 jit_solution(13881955935683165818)
XLA Ops:
  1.3 0.0 copy-start.4
  1.3 0.7 reshape.37.mean
  2.0 0.0 copy-done.4
  2.0 0.0 copy-start.5
  2.0 0.7 copy-done.5
  2.7 0.0 copy-start.6
  2.7 0.7 copy-done.6
  3.4 0.0 copy-start
  3.4 1.0 copy-done
  4.4 0.0 copy-start.1
  4.4 1.0 copy-done.1
  5.4 0.0 copy-start.2
  5.4 1.0 copy-done.2
  6.4 0.0 copy-start.3
  6.4 0.9 copy-done.3
  7.3 98.1 %shard_map.120 = (bf16[128,1536]{1,0:T(8,128)(2,1)S(1)}, f32[31,1536]{1,0:T(8,128)S(1)}, f32[1,1536]{1,0:T(1,128)S(1)}, f32[1,1536]{1,0:T(1,128)S(1)}) custom-call(s32[1]{0:T(128)S(6)} %copy.15.limit, bf16[128,1536]{1,0:T(8,128)(2,1)S(1)} %bitcast.4, bf16[128,1536]{1,0:T(8,128)(2,1)S(1)} %bitcast.5, bf16[48,3072]{1,0:T(8,128)(2,1)S(1)} %copy-done.2, ...), custom_call_target="tpu_custom_call" | custom-call | tf_op jit(solution)/shard_map/pallas_call | solution.py:283
  105.4 0.6 reduce
  106.0 0.6 reduce.1
  106.6 0.7 copy.16
  107.4 0.7 copy.17
  (3 shorter events, 0.0 us)
Async XLA Ops:
  1.3 0.7 copy-start.4
  2.0 0.7 copy-start.5
  2.7 0.7 copy-start.6
  3.4 1.0 copy-start
  4.4 1.0 copy-start.1
  5.4 1.0 copy-start.2
  6.4 0.9 copy-start.3

commit v2 on v1

v2 whole, which is shorter than its diff:
```python
import functools

import jax
import jax.numpy as jnp
from jax import lax
from jax.experimental import pallas as pl
from jax.experimental.pallas import tpu as pltpu
from jax.sharding import PartitionSpec as P

MESH = pl.DeviceIdType.MESH
D = 1536
KERNEL = 31
FRAMES = 2048
ROWS = 128
SPAN = 2 * ROWS
HALO = 32
GHALO = 16
WIDE = SPAN + 2 * HALO
MID = SPAN + 2 * GHALO
SHARD = 48
CW = 128
HALF = D // 2
CHUNKS = HALF // CW
DP, CHAN, TM = 16, 2, 16
GROUP = TM * CHAN
SUB = GROUP // 2
F32 = jnp.float32
BF16 = jnp.bfloat16
TILES = CHUNKS * 5
LAST = TILES - SUB


def copy_to(src, dst, send, recv, device):
    return pltpu.make_async_remote_copy(
        src_ref=src, dst_ref=dst, send_sem=send, recv_sem=recv, device_id=device, device_id_type=MESH
    )


def await_bytes(ref, sem):
    pltpu.make_async_copy(ref, ref, sem).wait()


def kernel(
    limit, x_in, og_in, w_in, ck_in, mean_in, var_in, gain_in, bias_in,
    out, kernel_out, gain_out, bias_out,
    wg, xe, oe, ck, vecs, rows, pre, gw, cg, near, pgr, acc, away, back, parts, rb1, rb2, res,
    in_sem, w_sem, pair_send, pair_recv, halo_send, halo_recv, opp_send, opp_recv, z_send, z_recv,
    y_send, y_recv, s_send, s_recv, r1_send, r1_recv, r2_send, r2_recv, r3_send, r3_recv,
    out_send, out_recv,
):
    dp, c, tm = lax.axis_index("dp"), lax.axis_index("chan"), lax.axis_index("tm")
    z, xh, y, xl = dp // 2, dp % 2, tm // 2, tm % 2
    opp_dp = dp + 1 - 2 * xh
    opposite = (opp_dp, c, tm + 1 - 2 * xl)
    partner = (dp, c, tm + 1 - 2 * xl)
    me = tm * CHAN + c
    mine = y * CHAN + c
    hb = y % 2

    def weight_cols(half, j):
        return pl.ds(pl.multiple_of(hb * D + half * HALF + j * CW, CW), CW)

    def own_rows(j):
        return pltpu.make_async_copy(
            w_in.at[:, weight_cols(xl, j)], wg.at[j, hb, dp, c], w_sem.at[j]
        )

    def fetch(j, carry):
        own_rows(j).start()
        return carry

    lax.fori_loop(0, CHUNKS, fetch, 0)
    own_at = pl.multiple_of(xl * ROWS, ROWS)
    here = pl.ds(own_at, ROWS)
    x_rows = xe.at[pl.ds(pl.multiple_of(HALO + xl * ROWS, HALO), ROWS)]
    og_rows = oe.at[pl.ds(pl.multiple_of(GHALO + xl * ROWS, GHALO), ROWS)]

    def half_cols(half):
        return pl.ds(pl.multiple_of(half * HALF, HALF), HALF)

    loads = [
        pltpu.make_async_copy(src, dst, in_sem.at[i])
        for i, (src, dst) in enumerate(
            (
                (x_in, x_rows),
                (og_in.at[:, half_cols(xl)], og_rows),
                (ck_in, ck),
                (mean_in, vecs.at[0]),
                (var_in, vecs.at[1]),
                (gain_in, vecs.at[2]),
                (bias_in, vecs.at[3]),
            )
        )
    ]
    for load in loads:
        load.start()

    barrier = pltpu.get_barrier_semaphore()

    def greet(i, carry):
        other = lax.rem(me + i, GROUP)
        pl.semaphore_signal(
            barrier, inc=1, device_id=(dp, other % 2, other // 2), device_id_type=MESH
        )
        return carry

    def greet_dp(i, carry):
        pl.semaphore_signal(
            barrier, inc=1, device_id=(lax.rem(dp + i, DP), c, tm), device_id_type=MESH
        )
        return carry

    pl.semaphore_signal(barrier, inc=1, device_id=opposite, device_id_type=MESH)
    lax.fori_loop(1, DP, greet_dp, 0)
    lax.fori_loop(1, GROUP, greet, 0)
    pl.semaphore_wait(barrier, GROUP + DP - 1)

    def to_opposite(j, carry):
        copy_to(
            w_in.at[:, weight_cols(1 - xl, j)], wg.at[j, hb, dp, c], opp_send, opp_recv, opposite
        ).start()
        return carry

    lax.fori_loop(0, CHUNKS, to_opposite, 0)

    def fetched(j, carry):
        own_rows(j).wait()
        return carry

    lax.fori_loop(0, CHUNKS, fetched, 0)

    up = (lax.rem(dp + 2, DP), c, tm)
    down = (lax.rem(dp + DP - 2, DP), c, tm)
    y_even = y + 1 - 2 * (y % 2)
    y_odd = lax.rem(y + 7 + 2 * (y % 2), 8)

    def ring_step(q, j, s):
        odd = j % 2
        sharer = (dp, c, (y_even * (1 - odd) + y_odd * odd) * 2 + xl)
        part = xh + q - 2 * q * xh
        for d, (steps, sign, device) in enumerate(((4 - odd, 7, up), (3 + odd, 1, down))):
            block = wg.at[j, hb, 2 * lax.rem(z + sign * s, 8) + part, c]

            @pl.when((s > 0) & (s <= steps))
            def _():
                await_bytes(block, z_recv.at[d, q, j, s - 1])

            @pl.when(s < steps)
            def _():
                copy_to(block, block, z_send.at[j], z_recv.at[d, q, j, s], device).start()

            @pl.when((s <= steps) & (s + 1 - d > 0))
            def _():
                copy_to(block, block, y_send.at[j], y_recv.at[j], sharer).start()

    def ring_steps(q, s):
        def one(j, carry):
            ring_step(q, j, s)
            return carry

        lax.fori_loop(0, CHUNKS, one, 0)

    ring_steps(0, 0)

    pair = (
        copy_to(x_in, x_rows, pair_send.at[0], pair_recv.at[0], partner),
        copy_to(
            og_in.at[:, half_cols(1 - xl)], og_rows, pair_send.at[1], pair_recv.at[1], partner
        ),
    )
    for p in pair:
        p.start()
    beyond = lax.rem(y + 7 + 2 * xl, 8) * 2
    x_edge = x_in.at[pl.ds(pl.multiple_of(xl * (ROWS - HALO), HALO), HALO)]
    x_far = xe.at[pl.ds(pl.multiple_of((1 - xl) * (HALO + SPAN), HALO), HALO)]
    og_edge = pl.ds(pl.multiple_of(xl * (ROWS - GHALO), GHALO), GHALO)
    og_far = oe.at[pl.ds(pl.multiple_of((1 - xl) * (GHALO + SPAN), GHALO), GHALO)]
    halos = []
    for other in range(2):
        device = (dp, c, beyond + other)
        halos.append(copy_to(x_edge, x_far, halo_send.at[other], halo_recv.at[xl], device))
        halos.append(
            copy_to(
                og_in.at[og_edge, other * HALF : (other + 1) * HALF], og_far,
                halo_send.at[2 + other], halo_recv.at[2 + xl], device,
            )
        )
    for h in halos:
        h.start()

    await_bytes(wg.at[:, hb, opp_dp, c], opp_recv)
    ring_steps(1, 0)
    for s in range(1, 5):
        for q in range(2):
            ring_steps(q, s)

    def relay(j):
        await_bytes(wg.at[j, 1 - hb, :, c], y_recv.at[j])
        block = wg.at[j, :, :, c]
        copy_to(block, block, s_send.at[j], s_recv.at[j], (dp, 1 - c, tm)).start()

    for load in loads:
        load.wait()
    for i in range(4):
        rows[i : i + 1] = vecs[i].reshape(1, D)
    rows[1:2] = 1.0 / jnp.sqrt(rows[1:2] + 1e-05)
    for p in pair:
        p.wait_recv()
    for side in range(2):
        await_bytes(xe.at[0:HALO], halo_recv.at[side])
        await_bytes(oe.at[0:GHALO], halo_recv.at[2 + side])
    t = lax.broadcasted_iota(jnp.int32, (WIDE, CW), 0) + (y * SPAN - HALO)
    keep = ((t >= 0) & (t < limit[0])).astype(F32)
    keep_mid = keep[HALO - GHALO : HALO + SPAN + GHALO]
    acc[...] = jnp.zeros_like(acc)

    def weights(j):
        return jnp.concatenate([wg[j, h].reshape(D, CW) for h in range(2)], axis=1)

    def channels(j):
        return pl.ds(pl.multiple_of(xl * HALF + j * CW, CW), CW)

    def forward(j):
        cs = channels(j)
        pre[j] = jnp.dot(xe[...], weights(j), preferred_element_type=F32)
        sg = lax.logistic(pre[j, :, CW:])
        gw[...] = (pre[j, :, :CW] * sg * keep).astype(BF16).astype(F32)
        pre[j, :, CW:] = sg
        mean, rstd, gain, bias = (rows[i : i + 1, cs] for i in range(4))
        scale = gain * rstd
        gs = jnp.zeros((8, CW), F32)
        bs = jnp.zeros((8, CW), F32)
        step = 96
        for r in range(0, MID, step):
            a = jnp.zeros((step, CW), F32)
            for k in range(KERNEL):
                a = a + ck[k : k + 1, cs] * gw[r + k + 1 : r + k + 1 + step, :]
            normed = (a - mean) * rstd
            act = normed * gain + bias
            sig = lax.logistic(act)
            ag = oe[r : r + step, pl.ds(pl.multiple_of(j * CW, CW), CW)].astype(F32)
            ag = ag * keep_mid[r : r + step] * sig * (1.0 + act * (1.0 - sig))
            cg[j, r : r + step] = (ag * scale).astype(BF16).astype(F32)
            lo, hi = max(r, GHALO) - r, min(r + step, GHALO + SPAN) - r
            gs = gs + jnp.sum((ag * normed)[lo:hi].reshape((hi - lo) // 8, 8, CW), axis=0)
            bs = bs + jnp.sum(ag[lo:hi].reshape((hi - lo) // 8, 8, CW), axis=0)
        sums = [jnp.zeros((8, CW), F32)] * KERNEL
        step = 64
        for r in range(0, SPAN, step):
            own = cg[j, GHALO + r : GHALO + r + step]
            for k in range(KERNEL):
                p = own * gw[r + k + 17 : r + k + 17 + step]
                sums[k] = sums[k] + jnp.sum(p.reshape(step // 8, 8, CW), axis=0)
        for k, total in enumerate(sums + [gs, bs]):
            parts[j, k : k + 1] = jnp.sum(total, axis=0, keepdims=True)
        parts[j, KERNEL + 2 :] = jnp.zeros((40 - KERNEL - 2, CW), F32)

        def give(i, carry):
            tile = 5 * j + i
            other, slot = lax.rem(tile, SUB), tile // SUB
            piece = parts.at[j, pl.ds(pl.multiple_of(8 * i, 8), 8)]

            @pl.when(other == mine)
            def _():
                rb1[slot, mine] = parts[j, pl.ds(pl.multiple_of(8 * i, 8), 8)]

            @pl.when(other != mine)
            def _():
                device = (dp, other % 2, (other // 2) * 2 + xl)
                copy_to(piece, rb1.at[slot, mine], r1_send, r1_recv.at[slot], device).start()

            return carry

        lax.fori_loop(0, 5, give, 0)

    def backward(j, first):
        cs = channels(j)
        near[...] = cg[j, pl.ds(pl.multiple_of(first, ROWS), ROWS + 2 * GHALO)]
        step = 64
        for r in range(0, ROWS, step):
            a = jnp.zeros((step, CW), F32)
            for k in range(KERNEL):
                a = a + ck[k : k + 1, cs] * near[r + 31 - k : r + 31 - k + step]
            t = lax.broadcasted_iota(jnp.int32, (step, CW), 0) + (y * SPAN + first + r)
            a = a * (t < limit[0]).astype(F32)
            at = pl.ds(pl.multiple_of(first + HALO + r, HALO), step)
            value, sg = pre[j, at, :CW], pre[j, at, CW:]
            a = a * sg
            pgr[r : r + step, :CW] = a.astype(BF16)
            pgr[r : r + step, CW:] = (a * value * (1.0 - sg)).astype(BF16)
        acc[pl.ds(pl.multiple_of(first, ROWS), ROWS)] += lax.dot_general(
            pgr[...], weights(j), (((1,), (1,)), ((), ())), preferred_element_type=F32
        )

    def backwards(lo, hi, first):
        def one(j, carry):
            backward(j, first)
            return carry

        lax.fori_loop(lo, hi, one, 0)

    def second(slot):
        await_bytes(rb1.at[slot, 0 : SUB - 1], r1_recv.at[slot])
        rb2[slot, dp] = jnp.sum(rb1[slot], axis=0)

        def spread(i, carry):
            piece = rb2.at[slot, dp]
            device = (lax.rem(dp + i, DP), c, tm)
            copy_to(piece, piece, r2_send.at[slot], r2_recv.at[slot], device).start()
            return carry

        lax.fori_loop(1, DP, spread, 0)

    def third(slot):
        await_bytes(rb2.at[slot, 0 : DP - 1], r2_recv.at[slot])
        index = xl * GROUP + slot * SUB + mine
        res[index] = jnp.sum(rb2[slot], axis=0) * (1.0 / 256.0)

        def share(i, carry):
            other = lax.rem(me + i, GROUP)
            piece = res.at[index]
            device = (dp, other % 2, other // 2)
            copy_to(piece, piece, r3_send.at[slot], r3_recv.at[slot], device).start()
            return carry

        lax.fori_loop(1, GROUP, share, 0)

    relay(0)
    relay(1)

    def chunk(j, carry):
        @pl.when(j + 2 < CHUNKS)
        def _():
            relay(j + 2)

        await_bytes(wg.at[j, :, :, 1 - c], s_recv.at[j])
        forward(j)
        return carry

    lax.fori_loop(0, CHUNKS, chunk, 0)

    there = pl.multiple_of((1 - xl) * ROWS, ROWS)
    second(0)
    backwards(0, CHUNKS // 2, there)

    @pl.when(mine < LAST)
    def _():
        second(1)

    backwards(CHUNKS // 2, CHUNKS, there)
    away[...] = acc[pl.ds(there, ROWS)].astype(BF16)
    give_back = copy_to(away, back, out_send, out_recv, partner)
    give_back.start()
    third(0)
    backwards(0, CHUNKS, own_at)

    @pl.when(mine < LAST)
    def _():
        third(1)

    give_back.wait()
    out[...] = (acc[here] + back[...].astype(F32)).astype(BF16)

    @pl.when(mine < LAST)
    def _():
        await_bytes(res.at[0 : 2 * LAST - 1], r3_recv.at[1])
        await_bytes(res.at[0 : TILES - 2], r1_send)
        await_bytes(rb2.at[1, 0 : DP - 1], r2_send.at[1])
        await_bytes(res.at[0 : GROUP - 1], r3_send.at[1])

    @pl.when(mine >= LAST)
    def _():
        await_bytes(res.at[0 : 2 * LAST], r3_recv.at[1])
        await_bytes(res.at[0 : TILES - 1], r1_send)

    await_bytes(res.at[0 : GROUP - 1], r3_recv.at[0])
    await_bytes(rb2.at[0, 0 : DP - 1], r2_send.at[0])
    await_bytes(res.at[0 : GROUP - 1], r3_send.at[0])
    for half in range(2):
        for j in range(CHUNKS):
            lo = half * HALF + j * CW
            cols = slice(lo, lo + CW)
            tile = half * GROUP + 5 * j
            for i in range(3):
                kernel_out[8 * i : 8 * i + 8, cols] = res[tile + i]
            kernel_out[24:KERNEL, cols] = res[tile + 3, 0:7]
            gain_out[:, cols] = res[tile + 3, 7:8]
            bias_out[:, cols] = res[tile + 4, 0:1]

    await_bytes(wg.at[:, hb, dp, c], opp_send)
    for p in pair:
        p.wait_send()
    for h in halos:
        h.wait_send()

    def sent(j, carry):
        await_bytes(wg.at[j, 0, 0:14, 0], z_send.at[j])
        await_bytes(wg.at[j, 0, :, 0], y_send.at[j])
        await_bytes(wg.at[j, :, :, c], s_send.at[j])
        return carry

    lax.fori_loop(0, CHUNKS, sent, 0)


def per_device(
    inputs, out_grad, proj_weight, conv_kernel, norm_mean, norm_var, norm_gain, norm_bias, lengths
):
    vmem = pl.BlockSpec(memory_space=pltpu.VMEM)
    dma = pltpu.SemaphoreType.DMA
    whole = pl.BlockSpec(memory_space=pltpu.HBM)
    grad, kernel_grad, gain_grad, bias_grad = pl.pallas_call(
        kernel,
        out_shape=(
            jax.ShapeDtypeStruct((ROWS, D), BF16),
            jax.ShapeDtypeStruct((KERNEL, D), F32),
            jax.ShapeDtypeStruct((1, D), F32),
            jax.ShapeDtypeStruct((1, D), F32),
        ),
        in_specs=[pl.BlockSpec(memory_space=pltpu.SMEM)] + [whole] * 8,
        out_specs=(vmem,) * 4,
        scratch_shapes=[
            pltpu.VMEM((CHUNKS, 2, DP, CHAN, SHARD, CW), BF16),
            pltpu.VMEM((WIDE, D), BF16),
            pltpu.VMEM((MID, HALF), BF16),
            pltpu.VMEM((KERNEL, D), F32),
            pltpu.VMEM((4, D), F32),
            pltpu.VMEM((8, D), F32),
            pltpu.VMEM((CHUNKS, WIDE, 2 * CW), F32),
            pltpu.VMEM((WIDE, CW), F32),
            pltpu.VMEM((CHUNKS, MID, CW), F32),
            pltpu.VMEM((ROWS + 2 * GHALO, CW), F32),
            pltpu.VMEM((ROWS, 2 * CW), BF16),
            pltpu.VMEM((SPAN, D), F32),
            pltpu.VMEM((ROWS, D), BF16),
            pltpu.VMEM((ROWS, D), BF16),
            pltpu.VMEM((CHUNKS, 40, CW), F32),
            pltpu.VMEM((2, SUB, 8, CW), F32),
            pltpu.VMEM((2, DP, 8, CW), F32),
            pltpu.VMEM((2 * GROUP, 8, CW), F32),
            dma((7,)), dma((CHUNKS,)),
            dma((2,)), dma((2,)),
            dma((4,)), dma((4,)),
            dma, dma,
            dma((CHUNKS,)), dma((2, 2, CHUNKS, 4)),
            dma((CHUNKS,)), dma((CHUNKS,)),
            dma((CHUNKS,)), dma((CHUNKS,)),
            dma, dma((2,)),
            dma((2,)), dma((2,)),
            dma((2,)), dma((2,)),
            dma, dma,
        ],
        compiler_params=pltpu.CompilerParams(
            collective_id=0, has_side_effects=True, vmem_limit_bytes=60 << 20
        ),
    )(
        lengths, inputs.reshape(ROWS, D), out_grad.reshape(ROWS, D), proj_weight, conv_kernel,
        norm_mean, norm_var, norm_gain, norm_bias,
    )
    return (
        grad.reshape(1, 1, ROWS, D),
        kernel_grad,
        gain_grad.reshape(D),
        bias_grad.reshape(D),
    )


def solution(mesh):
    in_specs = (
        P("dp", "chan", "tm", None),
        P("dp", "chan", "tm", None),
        P(("dp", "chan"), None),
        P(),
        P(),
        P(),
        P(),
        P(),
        P("dp"),
    )
    out_specs = (P("dp", "chan", "tm", None), P(), P(), P())
    return jax.shard_map(
        per_device, mesh=mesh, in_specs=in_specs, out_specs=out_specs, check_vma=False
    )
```

time: 108 us -> 71.2 us (0.66)
  Pallas kernels: 98.1 us -> 65.2 us
  local copies, waits for them, and re-layouts: 7.4 us -> 3.24 us
    pallas_call x1, Pallas kernels: 98.1 us -> 65.2 us  [per_device(): pl.pallas_call(kernel, out_shape=(jax.ShapeDtypeStruct((ROWS, D), BF16),...]
    unnamed x16 -> x8, local copies, waits for them, and re-layouts: 6.67 us -> 3.24 us
where the time goes in v2:
time: 71.2 us; the launch traced here: 71 us
  Pallas kernels  65.2 us (92%)
  local copies, waits for them, and re-layouts  3.24 us (5%)
  between operations  1.3 us (2%)
  other arithmetic  1.24 us (2%)
    pallas_call x1, Pallas kernels, per_device(): pl.pallas_call(kernel, out_shape=(jax.ShapeDtypeStruct((ROWS, D), BF16),...  65.2 us
    unnamed x8, local copies, waits for them, and re-layouts  3.24 us

profile of v2, /device:TPU:1, one launch (start us, length us, event | category | flops | bytes accessed | tf_op | source)
XLA Modules:
  0.0 71.0 jit_solution(12537545632168929386)
XLA Ops:
  1.3 65.2 %shard_map.120 = (bf16[128,1536]{1,0:T(8,128)(2,1)}, f32[31,1536]{1,0:T(8,128)}, f32[1,1536]{1,0:T(1,128)}, f32[1,1536]{1,0:T(1,128)}) custom-call(s32[1]{0:T(128)S(6)} %copy.15.limit, bf16[128,1536]{1,0:T(8,128)(2,1)} %bitcast.4, bf16[128,1536]{1,0:T(8,128)(2,1)} %bitcast.5, bf16[48,3072]{1,0:T(8,128)(2,1)} %w_in.1, f32[31,1536]{1,0:T(8,128)} %ck_in.1, ...), custom_call_target="tpu_custom_call" | custom-call | tf_op jit(solution)/shard_map/pallas_call | solution.py:411
  66.5 0.0 copy-start.2
  66.5 0.7 copy-done.2
  67.2 0.0 copy-start.1
  67.2 0.6 reduce
  67.8 0.1 copy-done.1
  67.9 0.6 reduce.1
  68.5 0.0 copy-start
  68.5 1.8 %copy.16 = bf16[1,1,128,1536]{3,2,1,0:T(8,128)(2,1)} copy(bf16[1,1,128,1536]{3,2,1,0:T(8,128)(2,1)} %bitcast.3) | data formatting | bytes 786432
  70.3 0.0 copy-done
  70.3 0.7 copy.17
Async XLA Ops:
  66.5 0.7 copy-start.2
  67.2 0.7 copy-start.1
  68.5 1.8 %copy-start = (f32[31,1536]{1,0:T(8,128)S(1)}, f32[31,1536]{1,0:T(8,128)}, u32[]{:S(2)}) copy-start(f32[31,1536]{1,0:T(8,128)} %get-tuple-element.17) | copy-start | bytes 571396

commit v3 on v2

--- a/solution.py
+++ b/solution.py
@@ -27,6 +27,7 @@
 F32 = jnp.float32
 BF16 = jnp.bfloat16
 TILES = CHUNKS * 5
+SET = CHUNKS // 2
 LAST = TILES - SUB
 
 
@@ -42,7 +43,7 @@
 
 def kernel(
     limit, x_in, og_in, w_in, ck_in, mean_in, var_in, gain_in, bias_in,
-    out, kernel_out, gain_out, bias_out,
+    out, sums_out,
     wg, xe, oe, ck, vecs, rows, pre, gw, cg, near, pgr, acc, away, back, parts, rb1, rb2, res,
     in_sem, w_sem, pair_send, pair_recv, halo_send, halo_recv, opp_send, opp_recv, z_send, z_recv,
     y_send, y_recv, s_send, s_recv, r1_send, r1_recv, r2_send, r2_recv, r3_send, r3_recv,
@@ -51,6 +52,7 @@
     dp, c, tm = lax.axis_index("dp"), lax.axis_index("chan"), lax.axis_index("tm")
     z, xh, y, xl = dp // 2, dp % 2, tm // 2, tm % 2
     opp_dp = dp + 1 - 2 * xh
+    hc = xl + xh - 2 * xl * xh
     opposite = (opp_dp, c, tm + 1 - 2 * xl)
     partner = (dp, c, tm + 1 - 2 * xl)
     me = tm * CHAN + c
@@ -62,7 +64,7 @@
 
     def own_rows(j):
         return pltpu.make_async_copy(
-            w_in.at[:, weight_cols(xl, j)], wg.at[j, hb, dp, c], w_sem.at[j]
+            w_in.at[:, weight_cols(hc, j)], wg.at[j, hb, dp, c], w_sem.at[j]
         )
 
     def fetch(j, carry):
@@ -83,7 +85,7 @@
         for i, (src, dst) in enumerate(
             (
                 (x_in, x_rows),
-                (og_in.at[:, half_cols(xl)], og_rows),
+                (og_in.at[:, half_cols(hc)], og_rows),
                 (ck_in, ck),
                 (mean_in, vecs.at[0]),
                 (var_in, vecs.at[1]),
@@ -95,6 +97,10 @@
     for load in loads:
         load.start()
 
+    def same_channels(i):
+        other = lax.rem(dp + i, DP)
+        return (other, c, 2 * y + hc + other % 2 - 2 * hc * (other % 2))
+
     barrier = pltpu.get_barrier_semaphore()
 
     def greet(i, carry):
@@ -105,23 +111,12 @@
         return carry
 
     def greet_dp(i, carry):
-        pl.semaphore_signal(
-            barrier, inc=1, device_id=(lax.rem(dp + i, DP), c, tm), device_id_type=MESH
-        )
+        pl.semaphore_signal(barrier, inc=1, device_id=same_channels(i), device_id_type=MESH)
         return carry
 
-    pl.semaphore_signal(barrier, inc=1, device_id=opposite, device_id_type=MESH)
     lax.fori_loop(1, DP, greet_dp, 0)
     lax.fori_loop(1, GROUP, greet, 0)
-    pl.semaphore_wait(barrier, GROUP + DP - 1)
-
-    def to_opposite(j, carry):
-        copy_to(
-            w_in.at[:, weight_cols(1 - xl, j)], wg.at[j, hb, dp, c], opp_send, opp_recv, opposite
-        ).start()
-        return carry
-
-    lax.fori_loop(0, CHUNKS, to_opposite, 0)
+    pl.semaphore_wait(barrier, GROUP + DP - 2)
 
     def fetched(j, carry):
         own_rows(j).wait()
@@ -134,38 +129,53 @@
     y_even = y + 1 - 2 * (y % 2)
     y_odd = lax.rem(y + 7 + 2 * (y % 2), 8)
 
-    def ring_step(q, j, s):
-        odd = j % 2
-        sharer = (dp, c, (y_even * (1 - odd) + y_odd * odd) * 2 + xl)
-        part = xh + q - 2 * q * xh
-        for d, (steps, sign, device) in enumerate(((4 - odd, 7, up), (3 + odd, 1, down))):
-            block = wg.at[j, hb, 2 * lax.rem(z + sign * s, 8) + part, c]
-
-            @pl.when((s > 0) & (s <= steps))
-            def _():
-                await_bytes(block, z_recv.at[d, q, j, s - 1])
-
-            @pl.when(s < steps)
-            def _():
-                copy_to(block, block, z_send.at[j], z_recv.at[d, q, j, s], device).start()
-
-            @pl.when((s <= steps) & (s + 1 - d > 0))
-            def _():
-                copy_to(block, block, y_send.at[j], y_recv.at[j], sharer).start()
-
-    def ring_steps(q, s):
-        def one(j, carry):
-            ring_step(q, j, s)
-            return carry
-
-        lax.fori_loop(0, CHUNKS, one, 0)
-
-    ring_steps(0, 0)
+    sibling = (dp, 1 - c, tm)
+    sharers = [(dp, c, other * 2 + xl) for other in (y_even, y_odd)]
+
+    def weight_block(g, dz, part):
+        return wg.at[g * SET : (g + 1) * SET, hb, 2 * lax.rem(z + dz, 8) + part, c]
+
+    def pass_on(block, g, d, q, s):
+        recv = y_recv.at[g, d, q, s]
+        copy_to(block, block, y_send.at[g], recv, sharers[g]).start()
+        copy_to(block, block, s_send.at[g], s_recv.at[g], sibling).start()
+
+    def ring_step(g, s):
+        for d, (steps, sign, device) in enumerate(((4 - g, 7, up), (3 + g, 1, down))):
+            block = weight_block(g, sign * s, xh)
+            if 0 < s <= steps:
+                await_bytes(block, z_recv.at[d, g, s - 1])
+            if s < steps:
+                copy_to(block, block, z_send.at[g], z_recv.at[d, g, s], device).start()
+            if s <= steps and s + 1 > d:
+                copy_to(block, block, opp_send.at[g], opp_recv.at[d, g, s], opposite).start()
+                pass_on(block, g, d, 0, s)
+
+    def opp_step(g, s):
+        for d, (steps, sign) in enumerate(((4 - g, 7), (3 + g, 1))):
+            if s <= steps and s + 1 > d:
+                block = weight_block(g, sign * s, 1 - xh)
+                await_bytes(block, opp_recv.at[d, g, s])
+                pass_on(block, g, d, 1, s)
+
+    def y_step(g, q, s):
+        for d, (steps, sign) in enumerate(((4 - g, 7), (3 + g, 1))):
+            if s <= steps and s + 1 > d:
+                dz = 2 * lax.rem(z + sign * s, 8) + (xh + q - 2 * q * xh)
+                block = wg.at[g * SET : (g + 1) * SET, 1 - hb, dz, c]
+                await_bytes(block, y_recv.at[g, d, q, s])
+                copy_to(block, block, s_send.at[g], s_recv.at[g], sibling).start()
+
+    def each(step, s):
+        for g in range(2):
+            step(g, s)
+
+    each(ring_step, 0)
 
     pair = (
         copy_to(x_in, x_rows, pair_send.at[0], pair_recv.at[0], partner),
         copy_to(
-            og_in.at[:, half_cols(1 - xl)], og_rows, pair_send.at[1], pair_recv.at[1], partner
+            og_in.at[:, half_cols(1 - hc)], og_rows, pair_send.at[1], pair_recv.at[1], partner
         ),
     )
     for p in pair:
@@ -181,23 +191,32 @@
         halos.append(copy_to(x_edge, x_far, halo_send.at[other], halo_recv.at[xl], device))
         halos.append(
             copy_to(
-                og_in.at[og_edge, other * HALF : (other + 1) * HALF], og_far,
+                og_in.at[og_edge, half_cols(xh if other == 0 else 1 - xh)], og_far,
                 halo_send.at[2 + other], halo_recv.at[2 + xl], device,
             )
         )
     for h in halos:
         h.start()
 
-    await_bytes(wg.at[:, hb, opp_dp, c], opp_recv)
-    ring_steps(1, 0)
-    for s in range(1, 5):
+    each(ring_step, 1)
+    for s in range(2, 5):
+        each(opp_step, s - 2)
+        each(ring_step, s)
         for q in range(2):
-            ring_steps(q, s)
-
-    def relay(j):
-        await_bytes(wg.at[j, 1 - hb, :, c], y_recv.at[j])
-        block = wg.at[j, :, :, c]
-        copy_to(block, block, s_send.at[j], s_recv.at[j], (dp, 1 - c, tm)).start()
+            if s - 2 - q >= 0:
+                each(lambda g, t, q=q: y_step(g, q, t), s - 2 - q)
+    each(opp_step, 3)
+    each(lambda g, t: y_step(g, 0, t), 3)
+    each(opp_step, 4)
+
+    def last_steps(g):
+        y_step(g, 1, 2)
+        y_step(g, 0, 4)
+        y_step(g, 1, 3)
+        y_step(g, 1, 4)
+
+    def await_sibling(g):
+        await_bytes(wg.at[g * SET : (g + 1) * SET, :, :, 1 - c], s_recv.at[g])
 
     for load in loads:
         load.wait()
@@ -218,7 +237,7 @@
         return jnp.concatenate([wg[j, h].reshape(D, CW) for h in range(2)], axis=1)
 
     def channels(j):
-        return pl.ds(pl.multiple_of(xl * HALF + j * CW, CW), CW)
+        return pl.ds(pl.multiple_of(hc * HALF + j * CW, CW), CW)
 
     def forward(j):
         cs = channels(j)
@@ -304,8 +323,9 @@
         rb2[slot, dp] = jnp.sum(rb1[slot], axis=0)
 
         def spread(i, carry):
+            i = DP // 2 + (2 * (i % 2) - 1) * (i // 2)
             piece = rb2.at[slot, dp]
-            device = (lax.rem(dp + i, DP), c, tm)
+            device = same_channels(i)
             copy_to(piece, piece, r2_send.at[slot], r2_recv.at[slot], device).start()
             return carry
 
@@ -313,11 +333,11 @@
 
     def third(slot):
         await_bytes(rb2.at[slot, 0 : DP - 1], r2_recv.at[slot])
-        index = xl * GROUP + slot * SUB + mine
+        index = hc * GROUP + slot * SUB + mine
         res[index] = jnp.sum(rb2[slot], axis=0) * (1.0 / 256.0)
 
         def share(i, carry):
-            other = lax.rem(me + i, GROUP)
+            other = lax.rem(me + SUB + (2 * (i % 2) - 1) * (i // 2), GROUP)
             piece = res.at[index]
             device = (dp, other % 2, other // 2)
             copy_to(piece, piece, r3_send.at[slot], r3_recv.at[slot], device).start()
@@ -325,15 +345,15 @@
 
         lax.fori_loop(1, GROUP, share, 0)
 
-    relay(0)
-    relay(1)
+    last_steps(0)
+    last_steps(1)
+    await_sibling(0)
 
     def chunk(j, carry):
-        @pl.when(j + 2 < CHUNKS)
+        @pl.when(j == SET)
         def _():
-            relay(j + 2)
-
-        await_bytes(wg.at[j, :, :, 1 - c], s_recv.at[j])
+            await_sibling(1)
+
         forward(j)
         return carry
 
@@ -376,30 +396,32 @@
     await_bytes(res.at[0 : GROUP - 1], r3_recv.at[0])
     await_bytes(rb2.at[0, 0 : DP - 1], r2_send.at[0])
     await_bytes(res.at[0 : GROUP - 1], r3_send.at[0])
+    sums_out[...] = res[...]
+
+    for p in pair:
+        p.wait_send()
+    for h in halos:
+        h.wait_send()
+
+    for g in range(2):
+        await_bytes(wg.at[0:SET, 0, 0:7, 0], z_send.at[g])
+        await_bytes(wg.at[0:SET, 0, 0:8, 0], opp_send.at[g])
+        await_bytes(wg.at[0:SET, 0, :, 0], y_send.at[g])
+        await_bytes(wg.at[0:SET, :, :, 0], s_send.at[g])
+
+
+def finish(grad, sums, out, kernel_out, gain_out, bias_out):
+    out[...] = grad[...]
     for half in range(2):
         for j in range(CHUNKS):
             lo = half * HALF + j * CW
             cols = slice(lo, lo + CW)
             tile = half * GROUP + 5 * j
             for i in range(3):
-                kernel_out[8 * i : 8 * i + 8, cols] = res[tile + i]
-            kernel_out[24:KERNEL, cols] = res[tile + 3, 0:7]
-            gain_out[:, cols] = res[tile + 3, 7:8]
-            bias_out[:, cols] = res[tile + 4, 0:1]
-
-    await_bytes(wg.at[:, hb, dp, c], opp_send)
-    for p in pair:
-        p.wait_send()
-    for h in halos:
-        h.wait_send()
-
-    def sent(j, carry):
-        await_bytes(wg.at[j, 0, 0:14, 0], z_send.at[j])
-        await_bytes(wg.at[j, 0, :, 0], y_send.at[j])
-        await_bytes(wg.at[j, :, :, c], s_send.at[j])
-        return carry
-
-    lax.fori_loop(0, CHUNKS, sent, 0)
+                kernel_out[8 * i : 8 * i + 8, cols] = sums[tile + i]
+            kernel_out[24:KERNEL, cols] = sums[tile + 3, 0:7]
+            gain_out[cols] = sums[tile + 3, 7]
+            bias_out[cols] = sums[tile + 4, 0]
 
 
 def per_device(
@@ -408,16 +430,14 @@
     vmem = pl.BlockSpec(memory_space=pltpu.VMEM)
     dma = pltpu.SemaphoreType.DMA
     whole = pl.BlockSpec(memory_space=pltpu.HBM)
-    grad, kernel_grad, gain_grad, bias_grad = pl.pallas_call(
+    grad, sums = pl.pallas_call(
         kernel,
         out_shape=(
             jax.ShapeDtypeStruct((ROWS, D), BF16),
-            jax.ShapeDtypeStruct((KERNEL, D), F32),
-            jax.ShapeDtypeStruct((1, D), F32),
-            jax.ShapeDtypeStruct((1, D), F32),
+            jax.ShapeDtypeStruct((2 * GROUP, 8, CW), F32),
         ),
         in_specs=[pl.BlockSpec(memory_space=pltpu.SMEM)] + [whole] * 8,
-        out_specs=(vmem,) * 4,
+        out_specs=(vmem,) * 2,
         scratch_shapes=[
             pltpu.VMEM((CHUNKS, 2, DP, CHAN, SHARD, CW), BF16),
             pltpu.VMEM((WIDE, D), BF16),
@@ -440,10 +460,10 @@
             dma((7,)), dma((CHUNKS,)),
             dma((2,)), dma((2,)),
             dma((4,)), dma((4,)),
-            dma, dma,
-            dma((CHUNKS,)), dma((2, 2, CHUNKS, 4)),
-            dma((CHUNKS,)), dma((CHUNKS,)),
-            dma((CHUNKS,)), dma((CHUNKS,)),
+            dma((2,)), dma((2, 2, 5)),
+            dma((2,)), dma((2, 2, 4)),
+            dma((2,)), dma((2, 2, 2, 5)),
+            dma((2,)), dma((2,)),
             dma, dma((2,)),
             dma((2,)), dma((2,)),
             dma((2,)), dma((2,)),
@@ -456,12 +476,16 @@
         lengths, inputs.reshape(ROWS, D), out_grad.reshape(ROWS, D), proj_weight, conv_kernel,
         norm_mean, norm_var, norm_gain, norm_bias,
     )
-    return (
-        grad.reshape(1, 1, ROWS, D),
-        kernel_grad,
-        gain_grad.reshape(D),
-        bias_grad.reshape(D),
-    )
+    grad, kernel_grad, gain_grad, bias_grad = pl.pallas_call(
+        finish,
+        out_shape=(
+            jax.ShapeDtypeStruct((ROWS, D), BF16),
+            jax.ShapeDtypeStruct((KERNEL, D), F32),
+            jax.ShapeDtypeStruct((D,), F32),
+            jax.ShapeDtypeStruct((D,), F32),
+        ),
+    )(grad, sums)
+    return grad.reshape(1, 1, ROWS, D), kernel_grad, gain_grad, bias_grad
 
 
 def solution(mesh):

time: 71.2 us -> 66.8 us (0.938)
  local copies, waits for them, and re-layouts: 3.24 us -> 0 us
  other arithmetic: 1.24 us -> 0 us
    unnamed x8 -> x0, local copies, waits for them, and re-layouts: 3.24 us -> none
    pallas_call x0 -> x1, Pallas kernels: none -> 1.9 us  [per_device(): pl.pallas_call(finish, out_shape=(jax.ShapeDtypeStruct((ROWS, D), BF16),...]
    pallas_call x1, Pallas kernels: 65.2 us -> 63.5 us  [per_device(): pl.pallas_call(kernel, out_shape=(jax.ShapeDtypeStruct((ROWS, D), BF16),...]
    pallas_call x2 -> x0, other arithmetic: 1.24 us -> none  [per_device(): pl.pallas_call(kernel, out_shape=(jax.ShapeDtypeStruct((ROWS, D), BF16),...]
where the time goes in v3:
time: 66.8 us; the launch traced here: 66.7 us
  Pallas kernels  65.4 us (98%)
  between operations  1.29 us (2%)
    pallas_call x1, Pallas kernels, per_device(): pl.pallas_call(kernel, out_shape=(jax.ShapeDtypeStruct((ROWS, D), BF16),...  63.5 us
    pallas_call x1, Pallas kernels, per_device(): pl.pallas_call(finish, out_shape=(jax.ShapeDtypeStruct((ROWS, D), BF16),...  1.9 us

profile of v3, /device:TPU:1, one launch (start us, length us, event | category | flops | bytes accessed | tf_op | source)
XLA Modules:
  0.0 66.7 jit_solution(8839511979800765123)
XLA Ops:
  1.3 63.5 %shard_map.120 = (bf16[128,1536]{1,0:T(8,128)(2,1)}, f32[64,8,128]{2,1,0:T(8,128)}) custom-call(s32[1]{0:T(128)S(6)} %copy.13.limit, bf16[128,1536]{1,0:T(8,128)(2,1)} %bitcast.3, bf16[128,1536]{1,0:T(8,128)(2,1)} %bitcast.4, bf16[48,3072]{1,0:T(8,128)(2,1)} %w_in.1, f32[31,1536]{1,0:T(8,128)} %ck_in.1, f32[1536]{0:T(1024)} %mean_in.1, f32[1536]{0:T(1024)} %var_in.1, ...), custom_call_target="tpu_custom_call" | custom-call | tf_op jit(solution)/shard_map/pallas_call | solution.py:433
  64.8 1.9 %shard_map.121 = (bf16[128,1536]{1,0:T(8,128)(2,1)}, f32[31,1536]{1,0:T(8,128)}, f32[1536]{0:T(1024)}, f32[1536]{0:T(1024)}) custom-call(bf16[128,1536]{1,0:T(8,128)(2,1)} %get-tuple-element.10.grad, f32[64,8,128]{2,1,0:T(8,128)} %get-tuple-element.11.sums), custom_call_target="tpu_custom_call" | custom-call | tf_op jit(solution)/shard_map/pallas_call | solution.py:479

commit v4 on v3

--- a/solution.py
+++ b/solution.py
@@ -27,6 +27,7 @@
 F32 = jnp.float32
 BF16 = jnp.bfloat16
 TILES = CHUNKS * 5
+PAIRS = CHUNKS // 2
 SET = CHUNKS // 2
 LAST = TILES - SUB
 
@@ -44,7 +45,7 @@
 def kernel(
     limit, x_in, og_in, w_in, ck_in, mean_in, var_in, gain_in, bias_in,
     out, sums_out,
-    wg, xe, oe, ck, vecs, rows, pre, gw, cg, near, pgr, acc, away, back, parts, rb1, rb2, res,
+    wg, xe, oe, ck, vecs, rows, pre_even, pre_odd, gw, cg, near, pgr, acc, away, back, parts, rb1, rb2, res,
     in_sem, w_sem, pair_send, pair_recv, halo_send, halo_recv, opp_send, opp_recv, z_send, z_recv,
     y_send, y_recv, s_send, s_recv, r1_send, r1_recv, r2_send, r2_recv, r3_send, r3_recv,
     out_send, out_recv,
@@ -239,12 +240,14 @@
     def channels(j):
         return pl.ds(pl.multiple_of(hc * HALF + j * CW, CW), CW)
 
-    def forward(j):
+    def project(pre, i, j):
+        pre[i] = jnp.dot(xe[...], weights(j), preferred_element_type=F32)
+
+    def forward(pre, i, j):
         cs = channels(j)
-        pre[j] = jnp.dot(xe[...], weights(j), preferred_element_type=F32)
-        sg = lax.logistic(pre[j, :, CW:])
-        gw[...] = (pre[j, :, :CW] * sg * keep).astype(BF16).astype(F32)
-        pre[j, :, CW:] = sg
+        sg = lax.logistic(pre[i, :, CW:])
+        gw[...] = (pre[i, :, :CW] * sg * keep).astype(BF16).astype(F32)
+        pre[i, :, CW:] = sg
         mean, rstd, gain, bias = (rows[i : i + 1, cs] for i in range(4))
         scale = gain * rstd
         gs = jnp.zeros((8, CW), F32)
@@ -292,7 +295,7 @@
 
         lax.fori_loop(0, 5, give, 0)
 
-    def backward(j, first):
+    def backward(pre, i, j, first):
         cs = channels(j)
         near[...] = cg[j, pl.ds(pl.multiple_of(first, ROWS), ROWS + 2 * GHALO)]
         step = 64
@@ -303,7 +306,7 @@
             t = lax.broadcasted_iota(jnp.int32, (step, CW), 0) + (y * SPAN + first + r)
             a = a * (t < limit[0]).astype(F32)
             at = pl.ds(pl.multiple_of(first + HALO + r, HALO), step)
-            value, sg = pre[j, at, :CW], pre[j, at, CW:]
+            value, sg = pre[i, at, :CW], pre[i, at, CW:]
             a = a * sg
             pgr[r : r + step, :CW] = a.astype(BF16)
             pgr[r : r + step, CW:] = (a * value * (1.0 - sg)).astype(BF16)
@@ -312,8 +315,9 @@
         )
 
     def backwards(lo, hi, first):
-        def one(j, carry):
-            backward(j, first)
+        def one(i, carry):
+            backward(pre_even, i, 2 * i, first)
+            backward(pre_odd, i, 2 * i + 1, first)
             return carry
 
         lax.fori_loop(lo, hi, one, 0)
@@ -349,34 +353,40 @@
     last_steps(1)
     await_sibling(0)
 
-    def chunk(j, carry):
-        @pl.when(j == SET)
+    def chunks(i, carry):
+        @pl.when(i == SET // 2)
         def _():
             await_sibling(1)
 
-        forward(j)
+        project(pre_odd, i, 2 * i + 1)
+        forward(pre_even, i, 2 * i)
+        project(pre_even, i + 1, jnp.minimum(2 * i + 2, CHUNKS - 1))
+        forward(pre_odd, i, 2 * i + 1)
         return carry
 
-    lax.fori_loop(0, CHUNKS, chunk, 0)
+    project(pre_even, 0, 0)
+    lax.fori_loop(0, PAIRS, chunks, 0)
 
     there = pl.multiple_of((1 - xl) * ROWS, ROWS)
     second(0)
-    backwards(0, CHUNKS // 2, there)
+    backwards(0, 1, there)
 
     @pl.when(mine < LAST)
     def _():
         second(1)
 
-    backwards(CHUNKS // 2, CHUNKS, there)
+    backwards(1, PAIRS, there)
     away[...] = acc[pl.ds(there, ROWS)].astype(BF16)
     give_back = copy_to(away, back, out_send, out_recv, partner)
     give_back.start()
     third(0)
-    backwards(0, CHUNKS, own_at)
+    backwards(0, 1, own_at)
 
     @pl.when(mine < LAST)
     def _():
         third(1)
+
+    backwards(1, PAIRS, own_at)
 
     give_back.wait()
     out[...] = (acc[here] + back[...].astype(F32)).astype(BF16)
@@ -445,7 +455,8 @@
             pltpu.VMEM((KERNEL, D), F32),
             pltpu.VMEM((4, D), F32),
             pltpu.VMEM((8, D), F32),
-            pltpu.VMEM((CHUNKS, WIDE, 2 * CW), F32),
+            pltpu.VMEM((PAIRS + 1, WIDE, 2 * CW), F32),
+            pltpu.VMEM((PAIRS, WIDE, 2 * CW), F32),
             pltpu.VMEM((WIDE, CW), F32),
             pltpu.VMEM((CHUNKS, MID, CW), F32),
             pltpu.VMEM((ROWS + 2 * GHALO, CW), F32),

time: 66.8 us -> 66.2 us (level)
  no operation moved by 1% of the time
where the time goes in v4:
time: 66.2 us; the launch traced here: 66 us
  Pallas kernels  64.8 us (98%)
  between operations  1.29 us (2%)
    pallas_call x1, Pallas kernels, per_device(): pl.pallas_call(kernel, out_shape=(jax.ShapeDtypeStruct((ROWS, D), BF16),...  62.9 us
    pallas_call x1, Pallas kernels, per_device(): pl.pallas_call(finish, out_shape=(jax.ShapeDtypeStruct((ROWS, D), BF16),...  1.9 us

profile of v4, /device:TPU:1, one launch (start us, length us, event | category | flops | bytes accessed | tf_op | source)
XLA Modules:
  0.0 66.0 jit_solution(4248447931333257398)
XLA Ops:
  1.3 62.9 %shard_map.120 = (bf16[128,1536]{1,0:T(8,128)(2,1)}, f32[64,8,128]{2,1,0:T(8,128)}) custom-call(s32[1]{0:T(128)S(6)} %copy.13.limit, bf16[128,1536]{1,0:T(8,128)(2,1)} %bitcast.3, bf16[128,1536]{1,0:T(8,128)(2,1)} %bitcast.4, bf16[48,3072]{1,0:T(8,128)(2,1)} %w_in.1, f32[31,1536]{1,0:T(8,128)} %ck_in.1, f32[1536]{0:T(1024)} %mean_in.1, f32[1536]{0:T(1024)} %var_in.1, ...), custom_call_target="tpu_custom_call" | custom-call | tf_op jit(solution)/shard_map/pallas_call | solution.py:443
  64.2 1.9 %shard_map.121 = (bf16[128,1536]{1,0:T(8,128)(2,1)}, f32[31,1536]{1,0:T(8,128)}, f32[1536]{0:T(1024)}, f32[1536]{0:T(1024)}) custom-call(bf16[128,1536]{1,0:T(8,128)(2,1)} %get-tuple-element.10.grad, f32[64,8,128]{2,1,0:T(8,128)} %get-tuple-element.11.sums), custom_call_target="tpu_custom_call" | custom-call | tf_op jit(solution)/shard_map/pallas_call | solution.py:490

commit v5 on v4

--- a/solution.py
+++ b/solution.py
@@ -350,7 +350,6 @@
         lax.fori_loop(1, GROUP, share, 0)
 
     last_steps(0)
-    last_steps(1)
     await_sibling(0)
 
     def chunks(i, carry):
@@ -365,6 +364,7 @@
         return carry
 
     project(pre_even, 0, 0)
+    last_steps(1)
     lax.fori_loop(0, PAIRS, chunks, 0)
 
     there = pl.multiple_of((1 - xl) * ROWS, ROWS)

time: 66.2 us -> 66.2 us (level)
  no operation moved by 1% of the time
where the time goes in v5:
time: 66.2 us; the launch traced here: 66 us
  Pallas kernels  64.7 us (98%)
  between operations  1.29 us (2%)
    pallas_call x1, Pallas kernels, per_device(): pl.pallas_call(kernel, out_shape=(jax.ShapeDtypeStruct((ROWS, D), BF16),...  62.8 us
    pallas_call x1, Pallas kernels, per_device(): pl.pallas_call(finish, out_shape=(jax.ShapeDtypeStruct((ROWS, D), BF16),...  1.9 us

profile of v5, /device:TPU:1, one launch (start us, length us, event | category | flops | bytes accessed | tf_op | source)
XLA Modules:
  0.0 66.0 jit_solution(8140083731681840133)
XLA Ops:
  1.3 62.8 %shard_map.120 = (bf16[128,1536]{1,0:T(8,128)(2,1)}, f32[64,8,128]{2,1,0:T(8,128)}) custom-call(s32[1]{0:T(128)S(6)} %copy.13.limit, bf16[128,1536]{1,0:T(8,128)(2,1)} %bitcast.3, bf16[128,1536]{1,0:T(8,128)(2,1)} %bitcast.4, bf16[48,3072]{1,0:T(8,128)(2,1)} %w_in.1, f32[31,1536]{1,0:T(8,128)} %ck_in.1, f32[1536]{0:T(1024)} %mean_in.1, f32[1536]{0:T(1024)} %var_in.1, ...), custom_call_target="tpu_custom_call" | custom-call | tf_op jit(solution)/shard_map/pallas_call | solution.py:443
  64.1 1.9 %shard_map.121 = (bf16[128,1536]{1,0:T(8,128)(2,1)}, f32[31,1536]{1,0:T(8,128)}, f32[1536]{0:T(1024)}, f32[1536]{0:T(1024)}) custom-call(bf16[128,1536]{1,0:T(8,128)(2,1)} %get-tuple-element.10.grad, f32[64,8,128]{2,1,0:T(8,128)} %get-tuple-element.11.sums), custom_call_target="tpu_custom_call" | custom-call | tf_op jit(solution)/shard_map/pallas_call | solution.py:490
